TPU v7x, 256 devices: a whole 4x4x8 slice. The times are simulated.
256 devices in a mesh: dp: 2 (over x_hi), head: 2 (over x_lo), row: 64 (over y, z, core).
Axes of the slice: x: 4 (x_hi: 2, x_lo: 2; x = x_hi * 2 + x_lo), y: 4, z: 8, core: 2. Of those that a mesh axis runs over, the one named last changes fastest.
Arguments:
- pair_act: bfloat16 [1024, 512, 128], P(('dp', 'row')), parts along dimension 0, may hold values from -12 to 12
- chain_id: int32 [1024], P('dp'), parts along dimension 0, may hold values from 0 to 3, never falling along the last dimension, each value on 1 to 256 neighbouring positions
- residue_mask: int32 [1024], P('dp'), parts along dimension 0, may hold values 0 or 1
- norm_gain: float32 [128], replicated, may hold values from 0.5 to 1.5
- w_proj: bfloat16 [128, 4, 128], P(None, 'head'), may hold values from -1.25 to 1.25
- w_bias: bfloat16 [128, 4], P(None, 'head'), may hold values from -0.9 to 0.9
- chain_bias: float32 [2, 4], P(None, 'head'), may hold values from -2 to 2
- w_out: bfloat16 [4, 32, 128], P('head'), may hold values from -0.5 to 0.5
- w_dist: bfloat16 [128, 64], replicated, may hold values from -0.5 to 0.5
- dist_bias: float32 [64], replicated, may hold values from -3 to 3
Outputs:
- new_pair: bfloat16 [1024, 512, 128], P(('dp', 'row')), parts along dimension 0
- distogram: bfloat16 [1024, 512, 64], P(('dp', 'row')), parts along dimension 0
There are 2 independent parts, one for each index of `dp`. A program takes and returns all parts, laid end to end along the dimension named above; an argument that names none is the same for every part. Nothing has to cross between parts.
Inputs may be any that keep to these rules, and one draw needn't show every extreme that they name: `chain_id`: chain ids never fall along the residues; no chain has more than half of the 512 residues.
All inputs are finite; a program needn't handle non-finite values.
Results may differ from a plain program's by a relative error of at most 0.013.
Values may be sent and summed in bfloat16 or wider, within the bound.
A program may use at most 64 MiB of HBM per device.

v0:
```python
import jax
import jax.numpy as jnp
from jax import lax
from jax.sharding import PartitionSpec as P


def normalize(values, gain_vec):
    values = values.astype(jnp.float32)
    center_val = jnp.mean(values, -1, keepdims=True)
    centered = values - center_val
    variance = jnp.mean(centered * centered, -1, keepdims=True)
    return centered * lax.rsqrt(variance + 1e-05) * gain_vec


def shards(
    pair_act,
    chain_id,
    residue_mask,
    norm_gain,
    w_proj,
    w_bias,
    chain_bias,
    w_out,
    w_dist,
    dist_bias,
):
    columns = lax.all_to_all(pair_act, "row", split_axis=1, concat_axis=0, tiled=True)
    normed = normalize(columns, norm_gain).astype(jnp.bfloat16)
    projected = jnp.einsum(
        "abc,chd->bahd", normed, w_proj, preferred_element_type=jnp.float32
    ).astype(jnp.bfloat16)
    local_bias = jnp.einsum(
        "abc,ch->hba", normed, w_bias, preferred_element_type=jnp.float32
    ).astype(jnp.bfloat16)
    bias_rows = lax.all_gather(local_bias, "row", axis=1, tiled=True)
    same_chain = chain_id[:, None] == chain_id[None, :]
    chain_term = jnp.where(
        same_chain[None], chain_bias[1][:, None, None], chain_bias[0][:, None, None]
    )
    mask_term = (residue_mask.astype(jnp.float32) - 1.0) * 1000000000.0
    total_bias = bias_rows.astype(jnp.float32) + chain_term + mask_term[None, None, :]
    head_size = w_out.shape[1]
    scaling = head_size ** (-0.5)

    def attend(tile_rows):
        queries = tile_rows[..., :head_size]
        keys_part = tile_rows[..., head_size : 2 * head_size]
        values_part = tile_rows[..., 2 * head_size : 3 * head_size]
        gate_part = tile_rows[..., 3 * head_size :]
        scores = (
            jnp.einsum("ihd,khd->hik", queries, keys_part, preferred_element_type=jnp.float32)
            * scaling
        )
        scores = scores + total_bias
        row_max = jnp.max(scores, -1, keepdims=True)
        weights = jnp.exp(scores - row_max)
        softmax_w = (weights / jnp.sum(weights, -1, keepdims=True)).astype(jnp.bfloat16)
        attended = jnp.einsum(
            "hik,khd->ihd", softmax_w, values_part, preferred_element_type=jnp.float32
        )
        return (jax.nn.sigmoid(gate_part.astype(jnp.float32)) * attended).astype(jnp.bfloat16)

    gated = lax.map(attend, projected)
    partial_sum = jnp.einsum("bihd,hdc->ibc", gated, w_out, preferred_element_type=jnp.float32)
    update = lax.psum(partial_sum.astype(jnp.bfloat16), "head").astype(jnp.float32)
    new_columns = (columns.astype(jnp.float32) + update).astype(jnp.bfloat16)
    new_rows = lax.all_to_all(new_columns, "row", split_axis=0, concat_axis=1, tiled=True)
    logits_rows = (
        jnp.dot(new_rows, w_dist, preferred_element_type=jnp.float32) + dist_bias
    ).astype(jnp.bfloat16)
    turned = lax.all_to_all(logits_rows, "row", split_axis=1, concat_axis=0, tiled=True)
    mirrored = jnp.transpose(turned, (1, 0, 2))
    distogram = (logits_rows.astype(jnp.float32) + mirrored.astype(jnp.float32)).astype(
        jnp.bfloat16
    )
    return (new_rows, distogram)


def solution(mesh):
    in_specs = (
        P(("dp", "row"), None, None),
        P("dp"),
        P("dp"),
        P(),
        P(None, "head", None),
        P(None, "head"),
        P(None, "head"),
        P("head", None, None),
        P(),
        P(),
    )
    out_specs = (P(("dp", "row"), None, None), P(("dp", "row"), None, None))
    return jax.shard_map(shards, mesh=mesh, in_specs=in_specs, out_specs=out_specs, check_vma=False)
```

profile of v0, /device:TPU:1, one launch (start us, length us, event | category | flops | bytes accessed | tf_op | source)
XLA Modules:
  0.0 305.4 jit_solution(1677374928414679372)
XLA Ops:
  7.2 1.9 copy.23
  9.1 41.5 %all_to_all.36 = bf16[8,512,128]{2,0,1:T(8,128)(2,1)S(1)} all-to-all(bf16[8,512,128]{2,0,1:T(8,128)(2,1)S(1)} %copy.23), channel_id=1, replica_groups=mesh['dp'=2,'head'=2,'row'=64] {'row'}, dimensions={1} | all-to-all | bytes 2097152 | tf_op jit(solution)/shard_map/all_to_all | solution.py:27
  50.9 0.6 bitcast_reduce_fusion
  51.6 1.3 fusion.14
  53.3 2.1 fusion.17
  55.8 3.0 convert_bitcast_fusion.1
  58.8 70.4 %all-gather.2.cloned.1.call-done = bf16[2,512,512]{2,0,1:T(2,128)(2,1)} async-done(((bf16[2,8,512]{2,0,1:T(2,128)(2,1)}), bf16[2,512,512]{2,0,1:T(2,128)(2,1)}) %all-gather.2.cloned.1.call-update) | async-done | bytes 1048592 | tf_op jit(solution)/shard_map/all_gather | solution.py:35
  129.2 2.9 add_add_fusion
  132.2 2.8 copy.27
  135.0 39.2 %while.10 = (s32[]{:T(128)}, bf16[8,512,2,32]{1,3,2,0:T(8,128)(2,1)}, bf16[8,512,2,128]{3,1,2,0:T(8,128)(2,1)}, f32[2,512,512]{1,2,0:T(8,128)}, s32[]{:T(128)}) while((s32[]{:T(128)}, bf16[8,512,2,32]{1,3,2,0:T(8,128)(2,1)}, bf16[8,512,2,128]{3,1,2,0:T(8,128)(2,1)}, f32[2,512,512]{1,2,0:T(8,128)}, s32[]{:T(128)}) %tuple.24), condition=%wide.region_5.6_spmd, body=%wide.region_2.5_spmd.sunk | while | flops 70977536 | bytes 11870785 | solution.py:63
  135.0 1.0 constant_dynamic-slice_fusion.2
  136.1 2.1 multiply_add_fusion.2
  138.2 0.5 fusion.44
  138.6 1.2 fusion.45
  139.9 1.0 constant_dynamic-slice_fusion.2
  141.0 2.1 multiply_add_fusion.2
  143.5 1.2 fusion.45
  144.8 1.0 constant_dynamic-slice_fusion.2
  145.9 2.1 multiply_add_fusion.2
  148.4 1.2 fusion.45
  149.7 1.0 constant_dynamic-slice_fusion.2
  150.8 2.1 multiply_add_fusion.2
  153.3 1.2 fusion.45
  154.6 1.0 constant_dynamic-slice_fusion.2
  155.7 2.1 multiply_add_fusion.2
  158.2 1.2 fusion.45
  159.5 1.0 constant_dynamic-slice_fusion.2
  160.6 2.1 multiply_add_fusion.2
  163.1 1.2 fusion.45
  164.3 1.0 constant_dynamic-slice_fusion.2
  165.5 2.1 multiply_add_fusion.2
  168.0 1.2 fusion.45
  169.2 1.0 constant_dynamic-slice_fusion.2
  170.4 2.1 multiply_add_fusion.2
  172.9 1.2 fusion.45
  174.1 2.5 fusion.15
  176.7 49.2 %all-reduce.2.cloned.1.call-done = bf16[512,8,128]{2,0,1:T(8,128)(2,1)} async-done(((bf16[512,8,128]{2,0,1:T(8,128)(2,1)}), bf16[512,8,128]{2,0,1:T(8,128)(2,1)}) %all-reduce.2.cloned.1.call-update) | async-done | bytes 1048592 | tf_op jit(solution)/shard_map/psum | solution.py:65
  225.8 1.5 fusion.12
  227.3 0.7 copy.28
  228.0 39.0 %all_to_all.37 = bf16[512,8,128]{2,1,0:T(8,128)(2,1)S(1)} all-to-all(bf16[512,8,128]{2,1,0:T(8,128)(2,1)S(1)} %copy.28), channel_id=1, replica_groups=mesh['dp'=2,'head'=2,'row'=64] {'row'}, dimensions={0} | all-to-all | bytes 2097152 | tf_op jit(solution)/shard_map/all_to_all | solution.py:67
  267.3 1.0 copy-done.1
  268.3 0.5 fusion.16
  268.7 0.8 copy.30
  269.5 0.7 reshape.88
  270.3 23.3 %all_to_all.38 = bf16[64,2,2048]{2,1,0:T(2,128)(2,1)S(1)} all-to-all(bf16[64,2,2048]{2,1,0:T(2,128)(2,1)S(1)} %reshape.88), channel_id=1, replica_groups=mesh['dp'=2,'head'=2,'row'=64] {'row'}, dimensions={0} | all-to-all | bytes 1048576 | tf_op jit(solution)/shard_map/all_to_all | solution.py:71
  293.6 0.7 reshape.89
  294.7 1.7 copy.33
  296.4 2.2 fusion.19
  (50 shorter events, 5.9 us)
Async XLA Ops:
  7.2 167.0 %copy-start = (bf16[2,32,128]{2,1,0:T(8,128)(2,1)S(1)}, bf16[2,32,128]{2,1,0:T(8,128)(2,1)}, u32[]{:S(2)}) copy-start(bf16[2,32,128]{2,1,0:T(8,128)(2,1)} %param.19) | copy-start | bytes 49156
  7.2 122.1 %all-gather.2.cloned.1.call-start = ((), (), s32[]{:S(2)}) async-start(), calls=%async_computation.3 | async-start | bytes 1064960 | tf_op jit(solution)/shard_map/all_gather | solution.py:35
  51.5 1.8 copy-start.8
  51.5 1.8 copy-start.9
  52.9 2.6 copy-start.5
  52.9 2.6 copy-start.4
  52.9 2.6 copy-start.3
  52.9 2.8 copy-start.7
  55.4 170.4 %all-reduce.2.cloned.1.call-start = ((), (), s32[]{:S(2)}) async-start(), calls=%async_computation.4 | async-start | bytes 2097152 | tf_op jit(solution)/shard_map/psum | solution.py:65
  228.0 40.2 %copy-start.2 = (bf16[128,64]{0,1:T(8,128)(2,1)S(1)}, bf16[128,64]{0,1:T(8,128)(2,1)}, u32[]{:S(2)}) copy-start(bf16[128,64]{0,1:T(8,128)(2,1)} %param.20) | copy-start | bytes 49156
  228.0 40.2 %copy-start.6 = (f32[64]{0:T(128)S(1)}, f32[64]{0:T(128)}, u32[]{:S(2)}) copy-start(f32[64]{0:T(128)} %param.21) | copy-start | bytes 772
  267.3 1.0 copy-start.1
Sparse Core Ops, SparseCore 0:
  55.5 73.6 all-gather.1
  176.8 48.9 all-reduce.1
where the time goes:
time: 306 us; the launch traced here: 305 us
  waiting for transfers between devices  120 us (39%)
  blocking collectives  104 us (34%)
  matrix products  34.6 us (11%)
  local copies, waits for them, and re-layouts  20 us (7%)
  between operations  14.3 us (5%)
  other arithmetic  12.8 us (4%)
    all_gather x1, waiting for transfers between devices, shards(): bias_rows = lax.all_gather(local_bias, 'row', axis=1, tiled=True)  70.4 us
    psum x1, waiting for transfers between devices, shards(): lax.psum(partial_sum.astype(jnp.bfloat16), 'head').astype(jnp.float32)  49.2 us
    all_to_all x1, blocking collectives, shards(): lax.all_to_all(pair_act, 'row', split_axis=1, concat_axis=0, tiled=True)  41.5 us
    all_to_all x1, blocking collectives, shards(): lax.all_to_all(new_columns, 'row', split_axis=0, concat_axis=1, tiled=True)  39 us
    all_to_all x1, blocking collectives, shards(): lax.all_to_all(logits_rows, 'row', split_axis=1, concat_axis=0, tiled=True)  23.3 us
    dot_general x8, matrix products, attend(): jnp.einsum('ihd,khd->hik', queries, keys_part, preferred_element_type=jnp...  16.6 us
    dot_general x8, matrix products, attend(): jnp.einsum('hik,khd->ihd', softmax_w, values_part, preferred_element_type...  9.95 us
    dynamic_slice x16, local copies, waits for them, and re-layouts, shards(): gated = lax.map(attend, projected)  8.9 us
  transfers between devices with their start and end apart: 2, of which 2 were waited for; matrix products, arithmetic and copies ran while one was open for 1% of the time, Pallas kernels for 0%

commit v1 on v0

v1 whole, which is shorter than its diff:
```python
import functools
import math

import jax
import jax.numpy as jnp
from jax import lax
from jax.experimental import pallas as pl
from jax.experimental.pallas import tpu as pltpu
from jax.sharding import PartitionSpec as P

MESH = pl.DeviceIdType.MESH
F32 = jnp.float32
BF16 = jnp.bfloat16
NT = (((1,), (1,)), ((), ()))
SCALE = 32.0**-0.5
SHAPE = {64: (4, 8), 8: (2, 2)}
PEERS_IN, BIAS_X, BIAS_Z, BIAS_Y, BIAS_C, W_P, W_O, OUT, FWD, LOG = 0, 2, 3, 4, 7, 8, 9, 10, 12, 14
N_SEM = 16


def layer_norm(values, gain):
    center = jnp.mean(values, -1, keepdims=True)
    centered = values - center
    variance = jnp.mean(centered * centered, -1, keepdims=True)
    return (centered * lax.rsqrt(variance + 1e-05) * gain).astype(BF16)


def kernel(
    ny,
    nz,
    x_ref,
    chain_ref,
    mask_ref,
    gain_ref,
    wproj_ref,
    wbias_ref,
    cbias_ref,
    wout_ref,
    wdist_ref,
    dbias_ref,
    new_ref,
    dist_ref,
    turn,
    xs,
    cols,
    gath,
    btab,
    bsc,
    wpg,
    wog,
    wre,
    wd2,
    qbuf,
    kbuf,
    vbuf,
    gbuf,
    pbuf,
    ns,
    rows,
    logc,
    ssem,
    rsem,
):
    nr = ny * nz * 2
    n = nr * 8
    ib = n // ny
    nb = nr // ny
    head = lax.axis_index("head")
    me = lax.axis_index("row")
    core = me % 2
    z = (me // 2) % nz
    y = me // (2 * nz)
    other = 1 - head

    def row_of(yy, zz, cc):
        return (yy * nz + zz) * 2 + cc

    def peer(idx):
        t = idx % nz
        rest = idx // nz
        sign = 2 * (t % 2) - 1
        dz = (sign * ((t + 1) // 2) + nz) % nz
        return row_of((y + rest // 2) % ny, (z + dz) % nz, (core + rest % 2) % 2)

    def to_row(src, dst, sem, target):
        return pltpu.make_async_remote_copy(
            src_ref=src,
            dst_ref=dst,
            send_sem=ssem.at[sem],
            recv_sem=rsem.at[sem],
            device_id={"row": target},
            device_id_type=MESH,
        )

    def to_other(src, dst, sem):
        return pltpu.make_async_remote_copy(
            src_ref=src,
            dst_ref=dst,
            send_sem=ssem.at[sem],
            recv_sem=rsem.at[sem],
            device_id={"head": other},
            device_id_type=MESH,
        )

    def wait_bytes(ref, sem):
        pltpu.make_async_copy(ref, ref, sem).wait()

    barrier = pltpu.get_barrier_semaphore()

    def greet(i, carry):
        pl.semaphore_signal(barrier, inc=1, device_id={"row": peer(i)}, device_id_type=MESH)
        return carry

    lax.fori_loop(1, nr, greet, 0)
    pl.semaphore_signal(barrier, inc=1, device_id={"head": other}, device_id_type=MESH)

    gain = gain_ref[...]

    def prepare(kk, carry):
        xk = x_ref[kk].astype(F32)
        turn[pl.ds(kk, n, stride=8), :] = xk
        nk = layer_norm(xk, gain)
        bk = lax.dot_general(wbias_ref[...], nk, NT, preferred_element_type=F32)
        bsc[0, pl.ds(kk, 1), :] = bk[0:1]
        bsc[1, pl.ds(kk, 1), :] = bk[1:2]
        return carry

    lax.fori_loop(0, 8, prepare, 0)
    def pick(i, carry):
        for hf in range(2):
            for j in range(nb // 2):
                r = i * (nb // 2) + j
                part = turn[pl.ds(pl.multiple_of(r * 64 + (4 * head + 2 * hf) * 8, 16), 16), :]
                xs[hf, r] = part.astype(BF16)
        return carry

    lax.fori_loop(0, 2 * ny, pick, 0)

    ids = chain_ref[...]
    lane = lax.broadcasted_iota(jnp.int32, (8, n), 1)
    sub = lax.broadcasted_iota(jnp.int32, (8, n), 0)
    mine = lane == sub + me * 8
    my_ids = jnp.sum(jnp.where(mine, ids, 0), -1, keepdims=True)
    my_mask = jnp.sum(jnp.where(mine, mask_ref[...], 0), -1, keepdims=True)
    mask_term = (my_mask.astype(F32) - 1.0) * 1000000000.0
    same = my_ids == ids
    blocks = []
    for hh in range(2):
        chain_term = jnp.where(same, cbias_ref[1, hh], cbias_ref[0, hh])
        blocks.append((bsc[hh] + chain_term + mask_term) * (1.0 / SCALE))
    gath[core, y, z, head] = jnp.concatenate(blocks, 0).astype(BF16)

    pl.semaphore_wait(barrier, nr)

    def send_cols(hf):
        def send(i, carry):
            q = peer(i)
            to_row(xs.at[hf, q], cols.at[hf, me], PEERS_IN + hf, q).start()
            return carry

        lax.fori_loop(1, nr, send, 0)
        pltpu.make_async_copy(xs.at[hf, me], cols.at[hf, me], rsem.at[PEERS_IN + hf]).start()

    own_block = gath.at[core, y, z, head]
    bias_x = to_other(own_block, own_block, BIAS_X)
    bias_x.start()
    w_p = to_other(wproj_ref, wpg, W_P)
    w_p.start()
    w_o = to_other(wout_ref, wog, W_O)
    w_o.start()
    send_cols(0)
    bias_x.wait()
    for d in range(1, nz):
        to_row(gath.at[core, y, z], gath.at[core, y, z], BIAS_Z, row_of(y, (z + d) % nz, core)).start()
    send_cols(1)
    sib = row_of(y, z, 1 - core)
    wait_bytes(gath.at[0, 0, pl.ds(0, nz - 1)], rsem.at[BIAS_Z])
    wait_bytes(gath.at[0, 0, pl.ds(0, nz - 1)], ssem.at[BIAS_Z])
    for d in range(1, ny):
        to_row(gath.at[core, y], gath.at[core, y], BIAS_Y + d - 1, row_of((y + d) % ny, z, core)).start()
    to_row(gath.at[core, y], gath.at[core, y], BIAS_C, sib).start()
    for d in range(1, ny):
        from_y = (y + ny - d) % ny
        wait_bytes(gath.at[core, from_y], rsem.at[BIAS_Y + d - 1])
        to_row(gath.at[core, from_y], gath.at[core, from_y], BIAS_C, sib).start()

    w_p.wait()
    w_o.wait()
    li = lax.broadcasted_iota(jnp.int32, (128, 128), 0)
    mi = lax.broadcasted_iota(jnp.int32, (128, 128), 1)
    for t in range(4):
        total = jnp.zeros((128, 128), F32)
        for hh in range(2):
            for which, ref in ((head, wproj_ref), (other, wpg)):
                h = 2 * which + hh
                pick = (mi // 32 == h) & (li == t * 32 + mi % 32)
                total += jnp.dot(
                    ref[:, hh * 128 : (hh + 1) * 128], pick.astype(BF16), preferred_element_type=F32
                )
        wre[t] = total.astype(BF16)
    wre[4, pl.ds(pl.multiple_of(head * 64, 64), 64), :] = wout_ref[...]
    wre[4, pl.ds(pl.multiple_of(other * 64, 64), 64), :] = wog[...]
    wd = wdist_ref[...].astype(F32)
    zero = jnp.zeros_like(wd)
    wd2[...] = jnp.concatenate(
        [jnp.concatenate([wd, zero], 1), jnp.concatenate([zero, wd], 1)], 0
    ).astype(BF16)
    db = dbias_ref[...]
    db2 = jnp.concatenate([db, db], 1)
    wide = lax.broadcasted_iota(jnp.int32, (n, 128), 1)
    for h in range(4):
        ones = jnp.where(wide // 32 == h, 1.0, 0.0).astype(BF16)
        for c in range(2):
            vbuf[c, h * n : (h + 1) * n, 128:] = ones

    def project(hf):
        def chunk(q, carry):
            at = pl.multiple_of(q * nb, nb)
            out = pl.ds(pl.multiple_of(q * ib, ib), ib)
            values = cols[hf, pl.ds(at, nb)].astype(F32).reshape(nb * 16, 128)
            normed = layer_norm(values, gain)
            for t in range(4):
                pt = jnp.dot(normed, wre[t], preferred_element_type=F32)
                pt = pt.reshape(nb, 2, 8, 128)
                for c in range(2):
                    val = pt[:, c].reshape(ib, 128)
                    if t == 0:
                        qbuf[c, out, :] = val.astype(BF16)
                    elif t == 1:
                        kbuf[c, out, :] = val.astype(BF16)
                    elif t == 2:
                        lanes = lax.broadcasted_iota(jnp.int32, (ib, 128), 1) // 32
                        for h in range(4):
                            vbuf[c, pl.ds(pl.multiple_of(h * n + q * ib, ib), ib), :128] = jnp.where(
                                lanes == h, val, 0.0
                            ).astype(BF16)
                    else:
                        gbuf[c, out, :] = jax.nn.sigmoid(val.astype(BF16).astype(F32))
            return carry

        lax.fori_loop(0, ny, chunk, 0)

    def repack(q, carry):
        at = pl.ds(pl.multiple_of(q * ib, ib), ib)
        for a in range(2):
            g0 = gath[0, q, :, a].astype(F32)
            g1 = gath[1, q, :, a].astype(F32)
            for hh in range(2):
                both = jnp.concatenate(
                    [g0[:, hh * 8 : hh * 8 + 8], g1[:, hh * 8 : hh * 8 + 8]], 1
                ).astype(BF16).reshape(ib, n)
                for b in range(ny):
                    btab[b, 2 * a + hh, at, :] = both[:, b * ib : (b + 1) * ib]
        return carry

    eye = (
        lax.broadcasted_iota(jnp.int32, (ib, ib), 0) == lax.broadcasted_iota(jnp.int32, (ib, ib), 1)
    ).astype(F32).astype(BF16)
    qlane = lax.broadcasted_iota(jnp.int32, (ib, 128), 1) // 32

    def attend(hf, b):
        at = pl.ds(pl.multiple_of(b * ib, ib), ib)
        blk = pl.ds(pl.multiple_of(b * nb, nb), nb)
        before = cols[hf, blk].astype(F32)
        after = []
        for c in range(2):
            q = qbuf[c, at, :]
            for h in range(4):
                qm = jnp.where(qlane == h, q, jnp.zeros_like(q))
                lhs = jnp.concatenate([qm, eye], 1)
                rhs = jnp.concatenate([kbuf[c], btab[b, h]], 1)
                s = lax.dot_general(lhs, rhs, NT, preferred_element_type=F32)
                top = jnp.max(s, -1, keepdims=True)
                pbuf[c, :, h * n : (h + 1) * n] = jnp.exp2(
                    (s - top) * (SCALE * math.log2(math.e))
                ).astype(BF16)
            nd = jnp.dot(pbuf[c], vbuf[c], preferred_element_type=F32)
            gated = (gbuf[c, at, :] * (nd[:, :128] / nd[:, 128:])).astype(BF16)
            upd = jnp.dot(gated, wre[4], preferred_element_type=F32)
            after.append(before[:, c * 8 : c * 8 + 8] + upd.reshape(nb, 8, 128))
        ns[hf, blk] = jnp.concatenate(after, 1).astype(BF16)
        flat = jnp.concatenate([v.reshape(ib, 128).astype(BF16) for v in after], 1)
        logits = jnp.dot(flat, wd2[...], preferred_element_type=F32) + db2
        logc[head, hf, at, :] = logits.astype(BF16)

    def forward(hf):
        wait_bytes(rows.at[head, hf], rsem.at[OUT + hf])
        to_other(rows.at[head, hf], rows.at[head, hf], FWD + hf).start()

    def half(hf, carry):
        wait_bytes(cols.at[hf], rsem.at[PEERS_IN + hf])
        project(hf)

        @pl.when(hf == 0)
        def _():
            wait_bytes(gath.at[0], rsem.at[BIAS_C])
            lax.fori_loop(0, ny, repack, 0)

        def step(t, c2):
            b = (y + t) % ny
            attend(hf, b)

            def send(j, c3):
                target = b * nb + (me % nb + j) % nb
                to_row(ns.at[hf, target], rows.at[head, hf, me], OUT + hf, target).start()
                return c3

            lax.fori_loop(jnp.where(t == 0, 1, 0), nb, send, 0)

            @pl.when(t == 0)
            def _():
                pltpu.make_async_copy(
                    ns.at[hf, me], rows.at[head, hf, me], rsem.at[OUT + hf]
                ).start()

            @pl.when((hf == 1) & (t == ny // 2))
            def _():
                forward(0)

            return c2

        lax.fori_loop(0, ny, step, 0)
        to_other(logc.at[head, hf], logc.at[head, hf], LOG + hf).start()
        return carry

    lax.fori_loop(0, 2, half, 0)
    forward(1)

    def place(a, hf):
        def block(i, carry):
            for j in range(nb // 2):
                r = i * (nb // 2) + j
                at = pl.ds(pl.multiple_of(r * 64 + (4 * a + 2 * hf) * 8, 16), 16)
                turn[at, :] = rows[a, hf, r].astype(F32)
            return carry

        lax.fori_loop(0, 2 * ny, block, 0)

    for hf in range(2):
        place(head, hf)
    for hf in range(2):
        wait_bytes(rows.at[other, hf], rsem.at[FWD + hf])
        place(other, hf)
        wait_bytes(logc.at[other, hf], rsem.at[LOG + hf])
    for kk in range(8):
        new = turn[pl.ds(kk, n, stride=8), :].astype(BF16)
        new_ref[kk] = new
        own = (jnp.dot(new, wdist_ref[...], preferred_element_type=F32) + db).astype(BF16)
        c = kk % 2
        mirrored = logc[kk // 4, (kk // 2) % 2][:, c * 64 : (c + 1) * 64]
        dist_ref[kk] = (own.astype(F32) + mirrored.astype(F32)).astype(BF16)

    for hf in range(2):
        wait_bytes(xs.at[hf, pl.ds(0, nr - 1)], ssem.at[PEERS_IN + hf])
        wait_bytes(xs.at[hf, pl.ds(0, nr - 1)], ssem.at[OUT + hf])
        wait_bytes(rows.at[head, hf], ssem.at[FWD + hf])
        wait_bytes(logc.at[head, hf], ssem.at[LOG + hf])
    for d in range(1, ny):
        wait_bytes(gath.at[core, y], ssem.at[BIAS_Y + d - 1])
    wait_bytes(gath.at[core], ssem.at[BIAS_C])


def shards(
    pair_act,
    chain_id,
    residue_mask,
    norm_gain,
    w_proj,
    w_bias,
    chain_bias,
    w_out,
    w_dist,
    dist_bias,
):
    _, n, width = pair_act.shape
    nr = n // 8
    ny, nz = SHAPE[nr]
    bins = w_dist.shape[1]
    ib = n // ny
    wb = jnp.zeros((16, width), BF16).at[:2].set(w_bias.T)
    vmem = pl.BlockSpec(memory_space=pltpu.VMEM)
    smem = pl.BlockSpec(memory_space=pltpu.SMEM)
    return pl.pallas_call(
        functools.partial(kernel, ny, nz),
        out_shape=(
            jax.ShapeDtypeStruct((8, n, width), BF16),
            jax.ShapeDtypeStruct((8, n, bins), BF16),
        ),
        in_specs=[vmem, vmem, vmem, vmem, vmem, vmem, smem, vmem, vmem, vmem],
        out_specs=(vmem, vmem),
        scratch_shapes=[
            pltpu.VMEM((n * 8, width), F32),
            pltpu.VMEM((2, nr, 16, width), BF16),
            pltpu.VMEM((2, nr, 16, width), BF16),
            pltpu.VMEM((2, ny, nz, 2, 16, n), BF16),
            pltpu.VMEM((ny, 4, n, ib), BF16),
            pltpu.VMEM((2, 8, n), F32),
            pltpu.VMEM((width, 256), BF16),
            pltpu.VMEM((64, width), BF16),
            pltpu.VMEM((5, width, width), BF16),
            pltpu.VMEM((2 * width, 2 * bins), BF16),
            pltpu.VMEM((2, n, width), BF16),
            pltpu.VMEM((2, n, width), BF16),
            pltpu.VMEM((2, 4 * n, 2 * width), BF16),
            pltpu.VMEM((2, n, width), F32),
            pltpu.VMEM((2, ib, 4 * n), BF16),
            pltpu.VMEM((2, nr, 16, width), BF16),
            pltpu.VMEM((2, 2, nr, 16, width), BF16),
            pltpu.VMEM((2, 2, n, 2 * bins), BF16),
            pltpu.SemaphoreType.DMA((N_SEM,)),
            pltpu.SemaphoreType.DMA((N_SEM,)),
        ],
        compiler_params=pltpu.CompilerParams(
            collective_id=0, has_side_effects=True, vmem_limit_bytes=48 << 20
        ),
        name="triangle",
    )(
        pair_act,
        chain_id.reshape(1, n),
        residue_mask.reshape(1, n),
        norm_gain.reshape(1, width),
        w_proj.reshape(width, 256),
        wb,
        chain_bias,
        w_out.reshape(64, width),
        w_dist,
        dist_bias.reshape(1, bins),
    )


def solution(mesh):
    in_specs = (
        P(("dp", "row"), None, None),
        P("dp"),
        P("dp"),
        P(),
        P(None, "head", None),
        P(None, "head"),
        P(None, "head"),
        P("head", None, None),
        P(),
        P(),
    )
    out_specs = (P(("dp", "row"), None, None), P(("dp", "row"), None, None))
    return jax.shard_map(shards, mesh=mesh, in_specs=in_specs, out_specs=out_specs, check_vma=False)
```

time: 306 us -> 85.2 us (0.28)
  waiting for transfers between devices: 120 us -> 0 us
  blocking collectives: 104 us -> 0 us
  Pallas kernels: 0 us -> 78.7 us
  matrix products: 34.6 us -> 0 us
  local copies, waits for them, and re-layouts: 20 us -> 5.54 us
  between operations: 14.3 us -> 0.72 us
  other arithmetic: 12.8 us -> 0 us
    all_to_all x3 -> x0, blocking collectives: 104 us -> none  [the longest x1 41.5 us: shards(): lax.all_to_all(pair_act, 'row', split_axis=1, concat_axis=0, tiled=True)]
    pallas_call x0 -> x1, Pallas kernels: none -> 78.7 us  [shards(): pl.pallas_call(functools.partial(kernel, ny, nz), out_shape=(jax.ShapeDty...]
    all_gather x1 -> x0, waiting for transfers between devices: 70.4 us -> none  [shards(): bias_rows = lax.all_gather(local_bias, 'row', axis=1, tiled=True)]
    psum x1 -> x0, waiting for transfers between devices: 49.2 us -> none  [shards(): lax.psum(partial_sum.astype(jnp.bfloat16), 'head').astype(jnp.float32)]
    dot_general x20 -> x0, matrix products: 34.6 us -> none  [the longest x8 16.6 us: attend(): jnp.einsum('ihd,khd->hik', queries, keys_part, preferred_element_type=jnp...]
    dynamic_slice x16 -> x0, local copies, waits for them, and re-layouts: 8.9 us -> none  [shards(): gated = lax.map(attend, projected)]
    convert_element_type x4 -> x0, other arithmetic: 4.07 us -> none  [the longest x1 2.18 us: shards(): (logits_rows.astype(jnp.float32) + mirrored.astype(jnp.float32)).astype(j...]
    sub x8 -> x0, other arithmetic: 3.6 us -> none  [attend(): weights = jnp.exp(scores - row_max)]
  transfers between devices with their start and end apart: 2 -> 0, of which waited for: 2 -> 0; matrix products, arithmetic and copies ran while one was open for 1% -> 0% of each run, Pallas kernels for 0% -> 0%
where the time goes in v1:
time: 85.2 us; the launch traced here: 84.9 us
  Pallas kernels  78.7 us (92%)
  local copies, waits for them, and re-layouts  5.54 us (7%)
    pallas_call x1, Pallas kernels, shards(): pl.pallas_call(functools.partial(kernel, ny, nz), out_shape=(jax.ShapeDty...  78.7 us
    unnamed x19, local copies, waits for them, and re-layouts  3.72 us

profile of v1, /device:TPU:1, one launch (start us, length us, event | category | flops | bytes accessed | tf_op | source)
XLA Modules:
  0.0 84.9 jit_solution(16129798795160403473)
XLA Ops:
  0.6 0.0 copy-start.7
  0.6 0.7 scatter.4.wbias_ref
  1.3 0.8 copy.12.wdist_ref
  2.2 0.0 copy-done.7
  2.2 0.0 copy-start.1
  2.2 0.0 copy-start.2
  2.2 0.0 copy-start.3
  2.2 0.0 copy-start.6
  2.2 0.0 copy-start.4
  2.2 0.0 copy-start.5
  2.3 0.6 copy-done.1
  2.9 0.0 copy-done.2
  2.9 0.0 copy-done.3
  2.9 0.0 copy-done.6
  2.9 0.0 copy-done.4
  2.9 0.0 copy-done.5
  2.9 0.0 copy-start
  2.9 1.2 %copy-done = bf16[8,512,128]{2,1,0:T(8,128)(2,1)S(1)} copy-done((bf16[8,512,128]{2,1,0:T(8,128)(2,1)S(1)}, bf16[8,512,128]{2,1,0:T(8,128)(2,1)}, u32[]{:S(2)}) %copy-start) | copy-done | bytes 1048600
  4.1 78.7 %triangle.1 = (bf16[8,512,128]{2,1,0:T(8,128)(2,1)S(1)}, bf16[8,512,64]{2,1,0:T(8,128)(2,1)S(1)}) custom-call(bf16[8,512,128]{2,1,0:T(8,128)(2,1)S(1)} %copy-done, s32[1,512]{1,0:T(1,128)S(1)} %bitcast.12, s32[1,512]{1,0:T(1,128)S(1)} %bitcast.13, f32[1,128]{1,0:T(1,128)S(1)} %bitcast.14, bf16[128,256]{1,0:T(8,128)(2,1)S(1)} %bitcast.10, ...), custom_call_target="tpu_custom_call" | custom-call | tf_op jit(solution)/shard_map/triangle/pallas_call | solution.py:383
  82.8 1.1 %copy.13 = bf16[8,512,64]{1,2,0:T(8,128)(2,1)} copy(bf16[8,512,64]{2,1,0:T(8,128)(2,1)S(1)} %get-tuple-element.15) | data formatting | bytes 1048576 | tf_op jit(solution)/shard_map/triangle/pallas_call | solution.py:383
  84.0 1.0 %copy.18 = bf16[8,512,128]{2,1,0:T(8,128)(2,1)} copy(bf16[8,512,128]{2,1,0:T(8,128)(2,1)S(1)} %get-tuple-element.18) | data formatting | bytes 2097152
  (1 shorter events, 0.0 us)
Async XLA Ops:
  0.6 1.5 %copy-start.7 = (bf16[128,2,128]{2,1,0:T(2,128)(2,1)S(1)}, bf16[128,2,128]{2,1,0:T(2,128)(2,1)}, u32[]{:S(2)}) copy-start(bf16[128,2,128]{2,1,0:T(2,128)(2,1)} %param.16) | copy-start | bytes 196612
  2.2 0.7 copy-start.1
  2.2 0.7 copy-start.2
  2.2 0.7 copy-start.3
  2.2 0.7 copy-start.6
  2.2 0.7 copy-start.4
  2.2 0.7 copy-start.5
  2.9 1.2 %copy-start = (bf16[8,512,128]{2,1,0:T(8,128)(2,1)S(1)}, bf16[8,512,128]{2,1,0:T(8,128)(2,1)}, u32[]{:S(2)}) copy-start(bf16[8,512,128]{2,1,0:T(8,128)(2,1)} %x_ref.1) | copy-start | bytes 3145732

commit v2 on v1

v2 whole, which is shorter than its diff:
```python
import functools
import math

import jax
import jax.numpy as jnp
from jax import lax
from jax.experimental import pallas as pl
from jax.experimental.pallas import tpu as pltpu
from jax.sharding import PartitionSpec as P

MESH = pl.DeviceIdType.MESH
F32 = jnp.float32
BF16 = jnp.bfloat16
NT = (((1,), (1,)), ((), ()))
TN = (((0,), (0,)), ((), ()))
SCALE = 32.0**-0.5
SHAPE = {64: (4, 8), 8: (2, 2)}
PEERS_IN, BIAS_Z, BIAS_Y, BIAS_X, BIAS_C, W_P, W_O, LOG, X_IN, OUT, FWD = 0, 4, 5, 17, 21, 25, 26, 27, 28, 29, 33
N_SEM = 37


def layer_norm(values, gain):
    center = jnp.mean(values, -1, keepdims=True)
    centered = values - center
    variance = jnp.mean(centered * centered, -1, keepdims=True)
    return (centered * lax.rsqrt(variance + 1e-05) * gain).astype(BF16)


def kernel(
    ny,
    nz,
    x_ref,
    chain_ref,
    mask_ref,
    gain_ref,
    wproj_ref,
    wbias_ref,
    cbias_ref,
    wout_ref,
    wdist_ref,
    dbias_ref,
    rows,
    logc,
    xbuf,
    turn,
    xs,
    cols,
    gath,
    btab,
    bsc,
    wpg,
    wog,
    wre,
    qbuf,
    kbuf,
    vbuf,
    gbuf,
    ns,
    own_log,
    ssem,
    rsem,
):
    nr = ny * nz * 2
    n = nr * 8
    ib = n // ny
    nb = nr // ny
    bins = wdist_ref.shape[0]
    head = lax.axis_index("head")
    me = lax.axis_index("row")
    core = me % 2
    z = (me // 2) % nz
    y = me // (2 * nz)
    other = 1 - head

    def row_of(yy, zz, cc):
        return (yy * nz + zz) * 2 + cc

    def peer(idx):
        t = idx % nz
        rest = idx // nz
        sign = 2 * (t % 2) - 1
        dz = (sign * ((t + 1) // 2) + nz) % nz
        return row_of((y + rest // 2) % ny, (z + dz) % nz, (core + rest % 2) % 2)

    def to_row(src, dst, sem, target):
        return pltpu.make_async_remote_copy(
            src_ref=src,
            dst_ref=dst,
            send_sem=ssem.at[sem],
            recv_sem=rsem.at[sem],
            device_id={"row": target},
            device_id_type=MESH,
        )

    def to_other(src, dst, sem):
        return pltpu.make_async_remote_copy(
            src_ref=src,
            dst_ref=dst,
            send_sem=ssem.at[sem],
            recv_sem=rsem.at[sem],
            device_id={"head": other},
            device_id_type=MESH,
        )

    def wait_bytes(ref, sem):
        pltpu.make_async_copy(ref, ref, sem).wait()

    pltpu.make_async_copy(x_ref, xbuf, rsem.at[X_IN]).start()

    barrier = pltpu.get_barrier_semaphore()

    def greet(i, carry):
        pl.semaphore_signal(barrier, inc=1, device_id={"row": peer(i)}, device_id_type=MESH)
        return carry

    lax.fori_loop(1, nr, greet, 0)
    pl.semaphore_signal(barrier, inc=1, device_id={"head": other}, device_id_type=MESH)

    gain = gain_ref[...]

    pltpu.make_async_copy(x_ref, xbuf, rsem.at[X_IN]).wait()

    def prepare(kk, carry):
        xk = xbuf[kk].astype(F32)
        turn[pl.ds(kk, n, stride=8), :] = xk
        nk = layer_norm(xk, gain)
        bk = lax.dot_general(wbias_ref[...], nk, NT, preferred_element_type=F32)
        bsc[0, pl.ds(kk, 1), :] = bk[0:1]
        bsc[1, pl.ds(kk, 1), :] = bk[1:2]
        return carry

    lax.fori_loop(0, 8, prepare, 0)
    def pick(i, carry):
        for j in range(nb // 2):
            r = i * (nb // 2) + j
            xs[r] = turn[pl.ds(pl.multiple_of(r * 64 + head * 32, 32), 32), :].astype(BF16)
        return carry

    lax.fori_loop(0, 2 * ny, pick, 0)

    ids = chain_ref[...]
    lane = lax.broadcasted_iota(jnp.int32, (8, n), 1)
    sub = lax.broadcasted_iota(jnp.int32, (8, n), 0)
    mine = lane == sub + me * 8
    my_ids = jnp.sum(jnp.where(mine, ids, 0), -1, keepdims=True)
    my_mask = jnp.sum(jnp.where(mine, mask_ref[...], 0), -1, keepdims=True)
    mask_term = (my_mask.astype(F32) - 1.0) * 1000000000.0
    same = my_ids == ids
    blocks = []
    for hh in range(2):
        chain_term = jnp.where(same, cbias_ref[1, hh], cbias_ref[0, hh])
        blocks.append((bsc[hh] + chain_term + mask_term) * (1.0 / SCALE))
    block = jnp.concatenate(blocks, 0).astype(BF16)
    for b in range(ny):
        gath[core, head, y, b, z] = block[:, b * ib : (b + 1) * ib]

    pl.semaphore_wait(barrier, nr)

    def send_cols(i, carry):
        q = peer(i)
        to_row(xs.at[q], cols.at[me], PEERS_IN + i // nb, q).start()
        return carry

    def bias_z():
        part = gath.at[core, head, y, :, z]
        for d in range(1, nz):
            to_row(part, part, BIAS_Z, row_of(y, (z + d) % nz, core)).start()

    def bias_y(t):
        for d in range(1, ny):
            part = gath.at[core, head, y, (y + d + t + 1) % ny]
            to_row(part, part, BIAS_Y + t * (ny - 1) + d - 1, row_of((y + d) % ny, z, core)).start()

    sib = row_of(y, z, 1 - core)

    def after_y(t):
        b = (y + t + 1) % ny
        for d in range(1, ny):
            wait_bytes(
                gath.at[core, head, (y + ny - d) % ny, b], rsem.at[BIAS_Y + t * (ny - 1) + d - 1]
            )
        part = gath.at[core, head, :, b]
        to_other(part, part, BIAS_X + t).start()
        to_row(part, part, BIAS_C + t, sib).start()

    def after_x(t):
        part = gath.at[core, other, :, (y + t + 1) % ny]
        wait_bytes(part, rsem.at[BIAS_X + t])
        to_row(part, part, BIAS_C + t, sib).start()

    bias_z()
    w_p = to_other(wproj_ref, wpg, W_P)
    w_p.start()
    w_o = to_other(wout_ref, wog, W_O)
    w_o.start()
    lax.fori_loop(1, nr, send_cols, 0)
    pltpu.make_async_copy(xs.at[me], cols.at[me], rsem.at[PEERS_IN]).start()

    li = lax.broadcasted_iota(jnp.int32, (128, 128), 0)
    mi = lax.broadcasted_iota(jnp.int32, (128, 128), 1)
    shift = li - mi
    mh = mi // 32
    ri = lax.broadcasted_iota(jnp.int32, (128, 256), 0) * 2
    rj = lax.broadcasted_iota(jnp.int32, (128, 256), 1)

    def arrange(which, ref):
        total = [jnp.zeros((128, 128), F32) for _ in range(4)]
        for hh in range(2):
            h = 2 * which + hh
            split = jnp.where(rj == ri + hh, 1.0, 0.0).astype(BF16)
            w = jnp.dot(split, ref[...], preferred_element_type=F32).astype(BF16)
            for t in range(4):
                pick = jnp.where((shift == 32 * (t - h)) & (mh == h), 1.0, 0.0).astype(BF16)
                total[t] += jnp.dot(w, pick, preferred_element_type=F32)
        return total

    mine_w = arrange(head, wproj_ref)
    for t in range(4):
        wre[t] = mine_w[t].astype(BF16)
    wre[4, pl.ds(pl.multiple_of(head * 64, 64), 64), :] = wout_ref[...]
    bi = lax.broadcasted_iota(jnp.int32, (bins, bins), 0)
    bj = lax.broadcasted_iota(jnp.int32, (bins, bins), 1)
    db = jnp.sum(jnp.where(bi == bj, dbias_ref[...], 0.0), -1, keepdims=True)
    for c in range(4):
        for pair in range(2):
            vbuf[c, pair, 64:, :] = jnp.ones((16, n), BF16)

    wait_bytes(gath.at[0, 0, 0, :, pl.ds(0, nz - 1)], rsem.at[BIAS_Z])
    for t in range(ny):
        bias_y(t)
    w_p.wait()
    w_o.wait()
    their_w = arrange(other, wpg)
    for t in range(4):
        full = wre[t].astype(F32) + their_w[t]
        wre[t] = (full if t == 1 else jnp.transpose(full)).astype(BF16)
    wre[4, pl.ds(pl.multiple_of(other * 64, 64), 64), :] = wog[...]
    after_y(0)
    after_y(1)
    after_x(0)

    def project():
        def chunk(d, carry):
            q = (y + ny - d) % ny
            wait_bytes(cols.at[pl.ds(q * nb, nb)], rsem.at[PEERS_IN + d])
            at = pl.multiple_of(q * nb, nb)
            out = pl.ds(pl.multiple_of(q * ib, ib), ib)
            values = cols[pl.ds(at, nb)].astype(F32).reshape(nb * 32, 128)
            normed = layer_norm(values, gain).astype(F32).reshape(nb, 4, 8, 128)
            for c in range(4):
                nc = normed[:, c].reshape(ib, 128).astype(BF16)
                kbuf[c, out, :] = jnp.dot(nc, wre[1], preferred_element_type=F32).astype(BF16)
                qt = lax.dot_general(wre[0], nc, NT, preferred_element_type=F32)
                qbuf[c, q] = qt.astype(BF16)
                vt = lax.dot_general(wre[2], nc, NT, preferred_element_type=F32).astype(BF16)
                for pair in range(2):
                    vbuf[c, pair, :64, out] = vt[pair * 64 : pair * 64 + 64]
                gt = lax.dot_general(wre[3], nc, NT, preferred_element_type=F32)
                gbuf[c, q] = jax.nn.sigmoid(gt.astype(BF16).astype(F32))
            return carry

        lax.fori_loop(0, ny, chunk, 0)

    def repack(b):
        def line(q, carry):
            at = pl.ds(pl.multiple_of(q * ib, ib), ib)
            for a in range(2):
                g0 = gath[0, a, q, b].astype(F32)
                g1 = gath[1, a, q, b].astype(F32)
                for hh in range(2):
                    both = jnp.concatenate([g0[:, hh * 8 : hh * 8 + 8], g1[:, hh * 8 : hh * 8 + 8]], 1)
                    btab[a, at, hh * ib : (hh + 1) * ib] = both.reshape(ib, ib)
            return carry

        lax.fori_loop(0, ny, line, 0)

    qrow = lax.broadcasted_iota(jnp.int32, (128, ib), 0) // 32

    def attend(b, hf):
        at = pl.ds(pl.multiple_of(b * ib, ib), ib)
        blk = pl.ds(pl.multiple_of(b * nb, nb), nb)
        sub16 = pl.ds(pl.multiple_of(hf * 16, 16), 16)
        before = cols[blk, sub16].astype(F32)
        units = [(cc, pair) for cc in range(2) for pair in range(2)]
        scores = []
        for cc, pair in units:
            qt = qbuf[hf * 2 + cc, b]
            rhs = jnp.concatenate(
                [jnp.where(qrow == 2 * pair + hh, qt, jnp.zeros_like(qt)) for hh in range(2)], 1
            )
            s = jnp.dot(kbuf[hf * 2 + cc], rhs, preferred_element_type=F32)
            scores.append(s + btab[pair])
        tops = [jnp.max(s, 0, keepdims=True) for s in scores]
        probs = [
            jnp.exp2((s - top) * (SCALE * math.log2(math.e))).astype(BF16)
            for s, top in zip(scores, tops)
        ]
        outs = [
            jnp.dot(vbuf[hf * 2 + cc, pair], p, preferred_element_type=F32)
            for (cc, pair), p in zip(units, probs)
        ]
        after = []
        for cc in range(2):
            c = hf * 2 + cc
            att = []
            for pair in range(2):
                o = outs[2 * cc + pair]
                for hh in range(2):
                    lanes = slice(hh * ib, (hh + 1) * ib)
                    att.append(o[hh * 32 : hh * 32 + 32, lanes] / o[64:65, lanes])
            gated = (gbuf[c, b] * jnp.concatenate(att, 0)).astype(BF16)
            upd = lax.dot_general(gated, wre[4], TN, preferred_element_type=F32)
            after.append(before[:, cc * 8 : cc * 8 + 8] + upd.reshape(nb, 8, 128))
        ns[blk, sub16] = jnp.concatenate(after, 1).astype(BF16)
        for cc in range(2):
            flat = after[cc].reshape(ib, 128).astype(BF16)
            logits = lax.dot_general(wdist_ref[...], flat, NT, preferred_element_type=F32) + db
            own_log[b, hf, cc * bins : (cc + 1) * bins, :] = logits.astype(BF16)

    def forward(t):
        part = rows.at[head, pl.ds(((y + 2 * ny - t - 1) % ny) * nb, nb)]
        wait_bytes(part, rsem.at[OUT + t])
        to_other(part, part, FWD + t).start()

    project()

    def step(t, carry):
        b = (y + t + 1) % ny

        @pl.when(t < ny - 2)
        def _():
            after_y(t + 2)

        @pl.when(t < ny - 1)
        def _():
            after_x(t + 1)

        wait_bytes(gath.at[1 - core, :, :, b], rsem.at[BIAS_C + t])
        repack(b)

        def two(hf, c2):
            attend(b, hf)

            @pl.when(t == ny - 1)
            def _():
                part = pl.ds(pl.multiple_of(hf * 16, 16), 16)

                def send_half(j, c3):
                    target = b * nb + (me % nb + j) % nb
                    to_row(
                        ns.at[target, part], rows.at[head, me, part], OUT + ny - 1, target
                    ).start()
                    return c3

                lax.fori_loop(1, nb, send_half, 0)

            return c2

        lax.fori_loop(0, 2, two, 0)

        def send(j, c3):
            target = b * nb + (me % nb + j) % nb
            to_row(ns.at[target], rows.at[head, me], OUT + t, target).start()
            return c3

        lax.fori_loop(0, jnp.where(t == ny - 1, 0, nb), send, 0)

        @pl.when(t == ny - 1)
        def _():
            pltpu.make_async_copy(ns.at[me], rows.at[head, me], rsem.at[OUT + ny - 1]).start()

        to_other(own_log.at[b], logc.at[head, b], LOG).start()
        pltpu.make_async_copy(own_log.at[b], logc.at[head, b], rsem.at[X_IN]).start()

        @pl.when(t >= 1)
        def _():
            forward(t - 1)

        return carry

    lax.fori_loop(0, ny, step, 0)
    forward(ny - 1)
    for t in range(ny):
        part = rows.at[other, pl.ds(((y + 2 * ny - t - 1) % ny) * nb, nb)]
        wait_bytes(part, rsem.at[FWD + t])
    wait_bytes(logc.at[other], rsem.at[LOG])
    wait_bytes(logc.at[head], rsem.at[X_IN])

    wait_bytes(xs.at[pl.ds(0, nb - 1)], ssem.at[PEERS_IN])
    for d in range(1, ny):
        wait_bytes(xs.at[pl.ds(0, nb)], ssem.at[PEERS_IN + d])
    for t in range(ny - 1):
        wait_bytes(ns.at[pl.ds(0, nb)], ssem.at[OUT + t])
    wait_bytes(ns.at[pl.ds(0, nb - 1)], ssem.at[OUT + ny - 1])
    for t in range(ny):
        wait_bytes(ns.at[pl.ds(0, nb)], ssem.at[FWD + t])
    wait_bytes(own_log, ssem.at[LOG])
    wait_bytes(gath.at[0, 0, 0, :, pl.ds(0, nz - 1)], ssem.at[BIAS_Z])
    for t in range(ny):
        for d in range(1, ny):
            wait_bytes(gath.at[core, head, y, 0], ssem.at[BIAS_Y + t * (ny - 1) + d - 1])
        wait_bytes(gath.at[core, head, :, 0], ssem.at[BIAS_X + t])
        wait_bytes(gath.at[core, :, :, 0], ssem.at[BIAS_C + t])


def finish(nb, rows_ref, logc_ref, wdist_ref, dbias_ref, new_ref, dist_ref, turn):
    bins = wdist_ref.shape[0]
    bi = lax.broadcasted_iota(jnp.int32, (bins, bins), 0)
    bj = lax.broadcasted_iota(jnp.int32, (bins, bins), 1)
    db = jnp.sum(jnp.where(bi == bj, dbias_ref[...], 0.0), -1, keepdims=True)
    for a in range(2):
        for r in range(nb):
            turn[r * 64 + a * 32 : r * 64 + a * 32 + 32, :] = rows_ref[a, r].astype(F32)
    for kk in range(8):
        new = turn[pl.ds(kk, nb * 8, stride=8), :].astype(BF16)
        new_ref[kk] = new
        own = (lax.dot_general(wdist_ref[...], new, NT, preferred_element_type=F32) + db).astype(BF16)
        c = kk % 2
        mirrored = logc_ref[kk // 4, 0, (kk // 2) % 2, c * bins : (c + 1) * bins, :]
        dist_ref[kk] = (own.astype(F32) + mirrored.astype(F32)).astype(BF16)


def shards(
    pair_act,
    chain_id,
    residue_mask,
    norm_gain,
    w_proj,
    w_bias,
    chain_bias,
    w_out,
    w_dist,
    dist_bias,
):
    _, n, width = pair_act.shape
    nr = n // 8
    ny, nz = SHAPE[nr]
    bins = w_dist.shape[1]
    ib = n // ny
    nb = nr // ny
    vmem = pl.BlockSpec(memory_space=pltpu.VMEM)
    smem = pl.BlockSpec(memory_space=pltpu.SMEM)
    hbm = pl.BlockSpec(memory_space=pl.ANY)
    wdist_t = w_dist.T
    dbias = dist_bias.reshape(1, bins)
    rows, logc = pl.pallas_call(
        functools.partial(kernel, ny, nz),
        out_shape=(
            jax.ShapeDtypeStruct((2, nr, 32, width), BF16),
            jax.ShapeDtypeStruct((2, ny, 2, 2 * bins, ib), BF16),
        ),
        in_specs=[hbm, vmem, vmem, vmem, vmem, vmem, smem, vmem, vmem, vmem],
        out_specs=(hbm, hbm),
        scratch_shapes=[
            pltpu.VMEM((8, n, width), BF16),
            pltpu.VMEM((n * 8, width), F32),
            pltpu.VMEM((nr, 32, width), BF16),
            pltpu.VMEM((nr, 32, width), BF16),
            pltpu.VMEM((2, 2, ny, ny, nz, 16, ib), BF16),
            pltpu.VMEM((2, n, 2 * ib), F32),
            pltpu.VMEM((2, 8, n), F32),
            pltpu.VMEM((2 * width, 128), BF16),
            pltpu.VMEM((64, width), BF16),
            pltpu.VMEM((5, width, width), BF16),
            pltpu.VMEM((4, ny, width, ib), BF16),
            pltpu.VMEM((4, n, width), BF16),
            pltpu.VMEM((4, 2, 80, n), BF16),
            pltpu.VMEM((4, ny, width, ib), F32),
            pltpu.VMEM((nr, 32, width), BF16),
            pltpu.VMEM((ny, 2, 2 * bins, ib), BF16),
            pltpu.SemaphoreType.DMA((N_SEM,)),
            pltpu.SemaphoreType.DMA((N_SEM,)),
        ],
        compiler_params=pltpu.CompilerParams(
            collective_id=0, has_side_effects=True, vmem_limit_bytes=60 << 20
        ),
        name="triangle",
    )(
        pair_act,
        chain_id.reshape(1, n),
        residue_mask.reshape(1, n),
        norm_gain.reshape(1, width),
        w_proj.reshape(2 * width, 128),
        w_bias.T,
        chain_bias,
        w_out.reshape(64, width),
        wdist_t,
        dbias,
    )
    new, dist = pl.pallas_call(
        functools.partial(finish, nb),
        grid=(ny,),
        out_shape=(
            jax.ShapeDtypeStruct((8, n, width), BF16),
            jax.ShapeDtypeStruct((8, bins, n), BF16),
        ),
        in_specs=[
            pl.BlockSpec((2, nb, 32, width), lambda q: (0, q, 0, 0)),
            pl.BlockSpec((2, 1, 2, 2 * bins, ib), lambda q: (0, q, 0, 0, 0)),
            pl.BlockSpec((bins, width), lambda q: (0, 0)),
            pl.BlockSpec((1, bins), lambda q: (0, 0)),
        ],
        out_specs=(
            pl.BlockSpec((8, ib, width), lambda q: (0, q, 0)),
            pl.BlockSpec((8, bins, ib), lambda q: (0, 0, q)),
        ),
        scratch_shapes=[pltpu.VMEM((nb * 64, width), F32)],
        compiler_params=pltpu.CompilerParams(vmem_limit_bytes=62 << 20),
        name="finish",
    )(rows, logc, wdist_t, dbias)
    return new, jnp.transpose(dist, (0, 2, 1))


def solution(mesh):
    in_specs = (
        P(("dp", "row"), None, None),
        P("dp"),
        P("dp"),
        P(),
        P(None, "head", None),
        P(None, "head"),
        P(None, "head"),
        P("head", None, None),
        P(),
        P(),
    )
    out_specs = (P(("dp", "row"), None, None), P(("dp", "row"), None, None))
    return jax.shard_map(shards, mesh=mesh, in_specs=in_specs, out_specs=out_specs, check_vma=False)
```

time: 85.2 us -> 68.1 us (0.80)
  Pallas kernels: 78.7 us -> 67.2 us
  local copies, waits for them, and re-layouts: 5.54 us -> 0 us
    pallas_call x1, Pallas kernels: 78.7 us -> 63.1 us  [shards(): pl.pallas_call(functools.partial(kernel, ny, nz), out_shape=(jax.ShapeDty...]
    pallas_call x0 -> x1, Pallas kernels: none -> 4.16 us  [shards(): pl.pallas_call(functools.partial(finish, nb), grid=(ny,), out_shape=(jax....]
    unnamed x19 -> x0, local copies, waits for them, and re-layouts: 3.72 us -> none
    pallas_call x1 -> x0, local copies, waits for them, and re-layouts: 1.13 us -> none  [shards(): pl.pallas_call(functools.partial(kernel, ny, nz), out_shape=(jax.ShapeDty...]
where the time goes in v2:
time: 68.1 us; the launch traced here: 67.9 us
  Pallas kernels  67.2 us (99%)
    pallas_call x1, Pallas kernels, shards(): pl.pallas_call(functools.partial(kernel, ny, nz), out_shape=(jax.ShapeDty...  63.1 us
    pallas_call x1, Pallas kernels, shards(): pl.pallas_call(functools.partial(finish, nb), grid=(ny,), out_shape=(jax....  4.16 us

profile of v2, /device:TPU:1, one launch (start us, length us, event | category | flops | bytes accessed | tf_op | source)
XLA Modules:
  0.0 67.9 jit_solution(10634917183364481453)
XLA Ops:
  0.6 63.1 %triangle.1 = (bf16[2,64,32,128]{3,2,1,0:T(8,128)(2,1)}, bf16[2,4,2,128,128]{4,3,2,1,0:T(8,128)(2,1)}) custom-call(bf16[8,512,128]{2,1,0:T(8,128)(2,1)} %x_ref.1, s32[1,512]{1,0:T(1,128)} %bitcast.13, s32[1,512]{1,0:T(1,128)} %bitcast.14, f32[1,128]{1,0:T(1,128)} %bitcast.17, bf16[256,128]{1,0:T(8,128)(2,1)} %bitcast.11, bf16[2,128]{1,0:T(2,128)(2,1)} %bitcast.18, ...), custom_call_target="tpu_custom_call" | custom-call | tf_op jit(solution)/shard_map/triangle/pallas_call | solution.py:446
  63.7 4.2 %finish.1 = (bf16[8,512,128]{2,1,0:T(8,128)(2,1)}, bf16[8,64,512]{2,1,0:T(8,128)(2,1)}) custom-call(bf16[2,64,32,128]{3,2,1,0:T(8,128)(2,1)} %get-tuple-element.6.rows_ref, bf16[2,4,2,128,128]{4,3,2,1,0:T(8,128)(2,1)} %get-tuple-element.7.logc_ref, bf16[64,128]{1,0:T(8,128)(2,1)} %bitcast.10, f32[1,64]{1,0:T(1,128)} %bitcast.16), custom_call_target="tpu_custom_call" | custom-call | tf_op jit(solution)/shard_map/finish/pallas_call | solution.py:490

commit v3 on v2

--- a/solution.py
+++ b/solution.py
@@ -15,8 +15,8 @@
 TN = (((0,), (0,)), ((), ()))
 SCALE = 32.0**-0.5
 SHAPE = {64: (4, 8), 8: (2, 2)}
-PEERS_IN, BIAS_Z, BIAS_Y, BIAS_X, BIAS_C, W_P, W_O, LOG, X_IN, OUT, FWD = 0, 4, 5, 17, 21, 25, 26, 27, 28, 29, 33
-N_SEM = 37
+PEERS_IN, BIAS_Z, BIAS_Y, BIAS_X, BIAS_C, W_P, W_O, LOG, X_IN, OUT, FWD = 0, 4, 5, 17, 21, 25, 26, 27, 28, 29, 34
+N_SEM = 38
 
 
 def layer_norm(values, gain):
@@ -59,6 +59,7 @@
     own_log,
     ssem,
     rsem,
+    ready,
 ):
     nr = ny * nz * 2
     n = nr * 8
@@ -109,11 +110,10 @@
 
     barrier = pltpu.get_barrier_semaphore()
 
-    def greet(i, carry):
-        pl.semaphore_signal(barrier, inc=1, device_id={"row": peer(i)}, device_id_type=MESH)
-        return carry
-
-    lax.fori_loop(1, nr, greet, 0)
+    near = [row_of(y, (z + d) % nz, core) for d in range(1, nz)]
+    cross = [row_of((y + i // 2) % ny, z, (core + i % 2) % 2) for i in range(1, 2 * ny)]
+    for p in near + cross:
+        pl.semaphore_signal(barrier, inc=1, device_id={"row": p}, device_id_type=MESH)
     pl.semaphore_signal(barrier, inc=1, device_id={"head": other}, device_id_type=MESH)
 
     gain = gain_ref[...]
@@ -130,6 +130,10 @@
         return carry
 
     lax.fori_loop(0, 8, prepare, 0)
+
+    pl.semaphore_wait(barrier, nz + 2 * ny - 1)
+    for p in cross:
+        pl.semaphore_signal(ready, inc=1, device_id={"row": p}, device_id_type=MESH)
     def pick(i, carry):
         for j in range(nb // 2):
             r = i * (nb // 2) + j
@@ -154,7 +158,7 @@
     for b in range(ny):
         gath[core, head, y, b, z] = block[:, b * ib : (b + 1) * ib]
 
-    pl.semaphore_wait(barrier, nr)
+    pl.semaphore_wait(ready, 2 * ny - 1)
 
     def send_cols(i, carry):
         q = peer(i)
@@ -173,15 +177,18 @@
 
     sib = row_of(y, z, 1 - core)
 
-    def after_y(t):
-        b = (y + t + 1) % ny
-        for d in range(1, ny):
-            wait_bytes(
-                gath.at[core, head, (y + ny - d) % ny, b], rsem.at[BIAS_Y + t * (ny - 1) + d - 1]
-            )
-        part = gath.at[core, head, :, b]
+    def pass_on(line, t):
+        part = gath.at[core, head, line, (y + t + 1) % ny]
         to_other(part, part, BIAS_X + t).start()
         to_row(part, part, BIAS_C + t, sib).start()
+
+    def after_y(t):
+        for d in range(1, ny):
+            line = (y + ny - d) % ny
+            wait_bytes(
+                gath.at[core, head, line, (y + t + 1) % ny], rsem.at[BIAS_Y + t * (ny - 1) + d - 1]
+            )
+            pass_on(line, t)
 
     def after_x(t):
         part = gath.at[core, other, :, (y + t + 1) % ny]
@@ -228,6 +235,8 @@
     wait_bytes(gath.at[0, 0, 0, :, pl.ds(0, nz - 1)], rsem.at[BIAS_Z])
     for t in range(ny):
         bias_y(t)
+    for t in range(ny):
+        pass_on(y, t)
     w_p.wait()
     w_o.wait()
     their_w = arrange(other, wpg)
@@ -327,18 +336,18 @@
     def step(t, carry):
         b = (y + t + 1) % ny
 
-        @pl.when(t < ny - 2)
-        def _():
-            after_y(t + 2)
-
-        @pl.when(t < ny - 1)
-        def _():
-            after_x(t + 1)
-
         wait_bytes(gath.at[1 - core, :, :, b], rsem.at[BIAS_C + t])
         repack(b)
 
         def two(hf, c2):
+            @pl.when((hf == 1) & (t < ny - 2))
+            def _():
+                after_y(t + 2)
+
+            @pl.when((hf == 1) & (t < ny - 1))
+            def _():
+                after_x(t + 1)
+
             attend(b, hf)
 
             @pl.when(t == ny - 1)
@@ -348,7 +357,7 @@
                 def send_half(j, c3):
                     target = b * nb + (me % nb + j) % nb
                     to_row(
-                        ns.at[target, part], rows.at[head, me, part], OUT + ny - 1, target
+                        ns.at[target, part], rows.at[head, me, part], OUT + ny - 1 + hf, target
                     ).start()
                     return c3
 
@@ -367,7 +376,11 @@
 
         @pl.when(t == ny - 1)
         def _():
-            pltpu.make_async_copy(ns.at[me], rows.at[head, me], rsem.at[OUT + ny - 1]).start()
+            for hf in range(2):
+                part = pl.ds(hf * 16, 16)
+                pltpu.make_async_copy(
+                    ns.at[me, part], rows.at[head, me, part], rsem.at[OUT + ny - 1 + hf]
+                ).start()
 
         to_other(own_log.at[b], logc.at[head, b], LOG).start()
         pltpu.make_async_copy(own_log.at[b], logc.at[head, b], rsem.at[X_IN]).start()
@@ -379,7 +392,10 @@
         return carry
 
     lax.fori_loop(0, ny, step, 0)
-    forward(ny - 1)
+    for hf in range(2):
+        part = rows.at[head, pl.ds(y * nb, nb), pl.ds(hf * 16, 16)]
+        wait_bytes(part, rsem.at[OUT + ny - 1 + hf])
+        to_other(part, part, FWD + ny - 1).start()
     for t in range(ny):
         part = rows.at[other, pl.ds(((y + 2 * ny - t - 1) % ny) * nb, nb)]
         wait_bytes(part, rsem.at[FWD + t])
@@ -391,7 +407,8 @@
         wait_bytes(xs.at[pl.ds(0, nb)], ssem.at[PEERS_IN + d])
     for t in range(ny - 1):
         wait_bytes(ns.at[pl.ds(0, nb)], ssem.at[OUT + t])
-    wait_bytes(ns.at[pl.ds(0, nb - 1)], ssem.at[OUT + ny - 1])
+    for hf in range(2):
+        wait_bytes(ns.at[pl.ds(0, nb - 1), pl.ds(0, 16)], ssem.at[OUT + ny - 1 + hf])
     for t in range(ny):
         wait_bytes(ns.at[pl.ds(0, nb)], ssem.at[FWD + t])
     wait_bytes(own_log, ssem.at[LOG])
@@ -411,13 +428,16 @@
     for a in range(2):
         for r in range(nb):
             turn[r * 64 + a * 32 : r * 64 + a * 32 + 32, :] = rows_ref[a, r].astype(F32)
+    news = [turn[pl.ds(kk, nb * 8, stride=8), :].astype(BF16) for kk in range(8)]
+    flat = jnp.concatenate(news, 0)
+    own = (lax.dot_general(wdist_ref[...], flat, NT, preferred_element_type=F32) + db).astype(BF16)
+    own = own.astype(F32)
     for kk in range(8):
-        new = turn[pl.ds(kk, nb * 8, stride=8), :].astype(BF16)
-        new_ref[kk] = new
-        own = (lax.dot_general(wdist_ref[...], new, NT, preferred_element_type=F32) + db).astype(BF16)
+        new_ref[kk] = news[kk]
         c = kk % 2
         mirrored = logc_ref[kk // 4, 0, (kk // 2) % 2, c * bins : (c + 1) * bins, :]
-        dist_ref[kk] = (own.astype(F32) + mirrored.astype(F32)).astype(BF16)
+        mine = own[:, kk * nb * 8 : (kk + 1) * nb * 8]
+        dist_ref[kk] = (mine + mirrored.astype(F32)).astype(BF16)
 
 
 def shards(
@@ -470,6 +490,7 @@
             pltpu.VMEM((ny, 2, 2 * bins, ib), BF16),
             pltpu.SemaphoreType.DMA((N_SEM,)),
             pltpu.SemaphoreType.DMA((N_SEM,)),
+            pltpu.SemaphoreType.REGULAR,
         ],
         compiler_params=pltpu.CompilerParams(
             collective_id=0, has_side_effects=True, vmem_limit_bytes=60 << 20

time: 68.1 us -> 66.1 us (0.971)
  Pallas kernels: 67.2 us -> 65.2 us
    pallas_call x1, Pallas kernels: 63.1 us -> 61.2 us  [shards(): pl.pallas_call(functools.partial(kernel, ny, nz), out_shape=(jax.ShapeDty...]
where the time goes in v3:
time: 66.1 us; the launch traced here: 65.8 us
  Pallas kernels  65.2 us (99%)
    pallas_call x1, Pallas kernels, shards(): pl.pallas_call(functools.partial(kernel, ny, nz), out_shape=(jax.ShapeDty...  61.2 us
    pallas_call x1, Pallas kernels, shards(): pl.pallas_call(functools.partial(finish, nb), grid=(ny,), out_shape=(jax....  4.04 us

profile of v3, /device:TPU:1, one launch (start us, length us, event | category | flops | bytes accessed | tf_op | source)
XLA Modules:
  0.0 65.8 jit_solution(13771964142014402011)
XLA Ops:
  0.6 61.2 %triangle.1 = (bf16[2,64,32,128]{3,2,1,0:T(8,128)(2,1)}, bf16[2,4,2,128,128]{4,3,2,1,0:T(8,128)(2,1)}) custom-call(bf16[8,512,128]{2,1,0:T(8,128)(2,1)} %x_ref.1, s32[1,512]{1,0:T(1,128)} %bitcast.13, s32[1,512]{1,0:T(1,128)} %bitcast.14, f32[1,128]{1,0:T(1,128)} %bitcast.17, bf16[256,128]{1,0:T(8,128)(2,1)} %bitcast.11, bf16[2,128]{1,0:T(2,128)(2,1)} %bitcast.18, ...), custom_call_target="tpu_custom_call" | custom-call | tf_op jit(solution)/shard_map/triangle/pallas_call | solution.py:466
  61.8 4.0 %finish.1 = (bf16[8,512,128]{2,1,0:T(8,128)(2,1)}, bf16[8,64,512]{2,1,0:T(8,128)(2,1)}) custom-call(bf16[2,64,32,128]{3,2,1,0:T(8,128)(2,1)} %get-tuple-element.6.rows_ref, bf16[2,4,2,128,128]{4,3,2,1,0:T(8,128)(2,1)} %get-tuple-element.7.logc_ref, bf16[64,128]{1,0:T(8,128)(2,1)} %bitcast.10, f32[1,64]{1,0:T(1,128)} %bitcast.16), custom_call_target="tpu_custom_call" | custom-call | tf_op jit(solution)/shard_map/finish/pallas_call | solution.py:511

commit v4 on v3

--- a/solution.py
+++ b/solution.py
@@ -350,29 +350,18 @@
 
             attend(b, hf)
 
-            @pl.when(t == ny - 1)
-            def _():
-                part = pl.ds(pl.multiple_of(hf * 16, 16), 16)
-
-                def send_half(j, c3):
-                    target = b * nb + (me % nb + j) % nb
-                    to_row(
-                        ns.at[target, part], rows.at[head, me, part], OUT + ny - 1 + hf, target
-                    ).start()
-                    return c3
-
-                lax.fori_loop(1, nb, send_half, 0)
-
+            part = pl.ds(pl.multiple_of(hf * 16, 16), 16)
+            sem = OUT + t + jnp.where(t == ny - 1, hf, 0)
+
+            def send_half(j, c3):
+                target = b * nb + (me % nb + j) % nb
+                to_row(ns.at[target, part], rows.at[head, me, part], sem, target).start()
+                return c3
+
+            lax.fori_loop(jnp.where(t == ny - 1, 1, 0), nb, send_half, 0)
             return c2
 
         lax.fori_loop(0, 2, two, 0)
-
-        def send(j, c3):
-            target = b * nb + (me % nb + j) % nb
-            to_row(ns.at[target], rows.at[head, me], OUT + t, target).start()
-            return c3
-
-        lax.fori_loop(0, jnp.where(t == ny - 1, 0, nb), send, 0)
 
         @pl.when(t == ny - 1)
         def _():

time: 66.1 us -> 65.4 us (0.989)
  Pallas kernels: 65.2 us -> 64.5 us
where the time goes in v4:
time: 65.4 us; the launch traced here: 65.2 us
  Pallas kernels  64.5 us (99%)
    pallas_call x1, Pallas kernels, shards(): pl.pallas_call(functools.partial(kernel, ny, nz), out_shape=(jax.ShapeDty...  60.5 us
    pallas_call x1, Pallas kernels, shards(): pl.pallas_call(functools.partial(finish, nb), grid=(ny,), out_shape=(jax....  4.04 us

profile of v4, /device:TPU:1, one launch (start us, length us, event | category | flops | bytes accessed | tf_op | source)
XLA Modules:
  0.0 65.2 jit_solution(14821788914086667536)
XLA Ops:
  0.6 60.5 %triangle.1 = (bf16[2,64,32,128]{3,2,1,0:T(8,128)(2,1)}, bf16[2,4,2,128,128]{4,3,2,1,0:T(8,128)(2,1)}) custom-call(bf16[8,512,128]{2,1,0:T(8,128)(2,1)} %x_ref.1, s32[1,512]{1,0:T(1,128)} %bitcast.13, s32[1,512]{1,0:T(1,128)} %bitcast.14, f32[1,128]{1,0:T(1,128)} %bitcast.17, bf16[256,128]{1,0:T(8,128)(2,1)} %bitcast.11, bf16[2,128]{1,0:T(2,128)(2,1)} %bitcast.18, ...), custom_call_target="tpu_custom_call" | custom-call | tf_op jit(solution)/shard_map/triangle/pallas_call | solution.py:455
  61.1 4.0 %finish.1 = (bf16[8,512,128]{2,1,0:T(8,128)(2,1)}, bf16[8,64,512]{2,1,0:T(8,128)(2,1)}) custom-call(bf16[2,64,32,128]{3,2,1,0:T(8,128)(2,1)} %get-tuple-element.6.rows_ref, bf16[2,4,2,128,128]{4,3,2,1,0:T(8,128)(2,1)} %get-tuple-element.7.logc_ref, bf16[64,128]{1,0:T(8,128)(2,1)} %bitcast.10, f32[1,64]{1,0:T(1,128)} %bitcast.16), custom_call_target="tpu_custom_call" | custom-call | tf_op jit(solution)/shard_map/finish/pallas_call | solution.py:500
